TPU v7x, 512 devices: a whole 4x4x16 slice. The times are simulated.
512 devices in a mesh: dp: 32 (over z_lo, x), tensor: 16 (over y, z_hi, core).
Axes of the slice: x: 4, y: 4, z: 16 (z_hi: 2, z_lo: 8; z = z_hi * 8 + z_lo), core: 2. Of those that a mesh axis runs over, the one named last changes fastest.
Arguments:
- x_panel: bfloat16 [16384, 4096], P('dp', 'tensor'), may hold values from -6 to 6
- grad_hidden: bfloat16 [16384, 14336], P('dp', 'tensor'), may hold values from -0.046875 to 0.046875
- gate_blocks: bfloat16 [112, 8, 128, 128], P('tensor'), may hold values from -0.1875 to 0.1875
- up_blocks: bfloat16 [112, 8, 128, 128], P('tensor'), may hold values from -0.1875 to 0.1875
- block_rows: int32 [112, 8], P('tensor'), may hold values from 0 to 31, as said below
- block_owner: int32 [112, 8], P('tensor'), may hold values from 0 to 31, as said below
Outputs:
- grad_owned: float32 [16, 32, 2, 2, 128, 128], P('tensor', 'dp')
Inputs may be any that keep to these rules, and one draw needn't show every extreme that they name: `block_rows`: the 8 block rows of one block column are distinct. `block_owner`: within each group of 7 consecutive block columns every dp index owns at most 2 blocks, and some index owns exactly 2.
All inputs are finite; a program needn't handle non-finite values.
Results may differ from a plain program's by a relative error of at most 0.013.
Values may be sent and summed in bfloat16 or wider, within the bound.
No kernel may reach another device: no remote copies, remote signals or barrier semaphores. Data moves between devices by JAX's collectives and lax.ppermute only.
A program may use at most 64 MiB of HBM per device.

v0:
```python
import jax
import jax.numpy as jnp
from jax import lax
from jax.sharding import PartitionSpec as P


def silu_parts(gate_pre):
    sigmoid_v = jax.nn.sigmoid(gate_pre)
    return (gate_pre * sigmoid_v, sigmoid_v * (1.0 + gate_pre * (1.0 - sigmoid_v)))


def body(x_panel, grad_hidden, gate_blocks, up_blocks, block_rows, block_owner):
    gathered = lax.all_gather(x_panel, "tensor", axis=1, tiled=True)
    token_count = gathered.shape[0]
    column_count = gate_blocks.shape[0]
    depth = gate_blocks.shape[1]
    block_size = gate_blocks.shape[2]
    row_total = gathered.shape[1] // block_size
    picked = gathered.reshape(token_count, row_total, block_size)[:, block_rows, :]
    gate_pre = jnp.einsum("tckb,ckbe->tce", picked, gate_blocks, preferred_element_type=jnp.float32)
    up_pre = jnp.einsum("tckb,ckbe->tce", picked, up_blocks, preferred_element_type=jnp.float32)
    activation, derivative = silu_parts(gate_pre)
    grad_f32 = grad_hidden.reshape(token_count, column_count, block_size).astype(jnp.float32)
    grad_gate_act = (grad_f32 * up_pre * derivative).astype(jnp.bfloat16)
    grad_up_act = (grad_f32 * activation).astype(jnp.bfloat16)
    paired = jnp.stack([grad_gate_act, grad_up_act], 2)
    partial_value = jnp.einsum(
        "tckb,tcme->ckmbe", picked, paired, preferred_element_type=jnp.float32
    )
    partial_value = partial_value.astype(jnp.bfloat16)
    owner_count = lax.axis_size("dp")
    block_count = column_count * depth
    capacity = block_count // owner_count + 1
    flat_owner = block_owner.reshape(block_count)
    onehot = (flat_owner[:, None] == jnp.arange(owner_count, dtype=jnp.int32)[None, :]).astype(
        jnp.int32
    )
    before = jnp.cumsum(onehot, 0) - onehot
    slot_index = jnp.sum(onehot * before, 1)
    target = flat_owner * capacity + slot_index
    packed = jnp.zeros((owner_count * capacity, 2, block_size, block_size), jnp.bfloat16)
    packed = packed.at[target].set(partial_value.reshape(block_count, 2, block_size, block_size))
    arrived = lax.all_to_all(
        packed.reshape(owner_count, capacity, 2, block_size, block_size),
        "dp",
        split_axis=0,
        concat_axis=0,
        tiled=True,
    )
    summed = jnp.sum(arrived.astype(jnp.float32), 0)
    return summed.reshape(1, 1, capacity, 2, block_size, block_size)


def solution(mesh):
    in_specs = (
        P("dp", "tensor"),
        P("dp", "tensor"),
        P("tensor", None, None, None),
        P("tensor", None, None, None),
        P("tensor", None),
        P("tensor", None),
    )
    out_specs = P("tensor", "dp", None, None, None, None)
    return jax.shard_map(body, mesh=mesh, in_specs=in_specs, out_specs=out_specs, check_vma=False)
```

profile of v0, /device:TPU:8, one launch (start us, length us, event | category | flops | bytes accessed | tf_op | source)
XLA Modules:
  0.0 384.3 jit_solution(14458488507015758200)
XLA Ops:
  6.5 0.0 copy-start
  6.5 0.0 all-gather.2.cloned.1.call-start
  6.5 1.9 copy.22
  8.5 0.0 all-gather.2.cloned.1.call-update
  8.5 0.7 compare_select_fusion
  9.2 0.1 reshape.52
  9.3 1.5 copy.21
  10.7 0.0 copy-start.3
  10.7 1.6 copy.24
  12.3 0.0 copy-done.3
  12.3 0.1 eq.15
  12.4 0.1 mul.39
  12.5 0.1 fusion.12
  12.6 0.1 reduce_window_sum.11
  12.7 0.2 select_reduce_fusion
  12.9 120.1 %all-gather.2.cloned.1.call-done = bf16[512,4096]{0,1:T(8,128)(2,1)} async-done(((bf16[512,256]{0,1:T(8,128)(2,1)}), bf16[512,4096]{0,1:T(8,128)(2,1)}) %all-gather.2.cloned.1.call-update) | async-done | bytes 4194320 | tf_op jit(solution)/shard_map/all_gather | solution.py:13
  132.9 6.4 %copy.23 = bf16[512,32,128]{2,0,1:T(8,128)(2,1)} copy(bf16[512,32,128]{0,2,1:T(8,128)(2,1)} %bitcast.81) | data formatting | bytes 8388608 | tf_op jit(solution)/shard_map/reshape | solution.py:19
  139.4 7.4 %gather_fusion = bf16[56,512,128]{2,1,0:T(8,128)(2,1)} fusion(bf16[512,32,128]{2,0,1:T(8,128)(2,1)} %copy.23, s32[1024]{0:T(1024)S(1)} %pad_clamp_fusion), kind=kCustom, calls=%fused_computation | custom fusion | bytes 14680288 | tf_op jit(solution)/shard_map/gather | solution.py:19
  146.8 0.0 copy-done
  146.9 5.3 %fusion.14 = f32[7,512,128,1]{2,1,3,0:T(8,128)S(1)} fusion(bf16[512,7,8,128]{3,0,2,1:T(8,128)(2,1)} %bitcast.78, bf16[7,8,128,128]{3,2,1,0:T(8,128)(2,1)S(1)} %copy-done), kind=kOutput, calls=%fused_computation.30 | convolution fusion | flops 939524096 | bytes 11010048 | tf_op jit(solution)/shard_map/tckb,ckbe->tce/dot_general | solution.py:20
  152.1 0.0 copy-done.1
  152.2 0.0 copy-start.4
  152.2 0.5 fusion.11
  152.7 0.0 copy-done.2
  152.7 1.1 copy-done.4
  153.8 2.1 fusion.10
  155.9 3.9 %convert_bitcast_fusion = bf16[7,8,2,128,128]{3,4,1,2,0:T(8,128)(2,1)} fusion(bf16[512,7,8,128,1]{3,0,2,4,1:T(8,128)(2,1)S(1)} %bitcast.80, bf16[512,7,1,128]{3,0,1,2:T(8,128)(2,1)S(1)} %fusion.11, bf16[512,7,1,128]{3,0,1,2:T(8,128)(2,1)S(1)} %fusion.10), kind=kOutput, calls=%fused_computation.3 | convolution fusion | flops 1881800704 | bytes 12845056 | tf_op jit(solution)/shard_map/tckb,tcme->ckmbe/dot_general | solution.py:27
  159.8 6.2 %copy.27 = bf16[7,8,2,128,128]{4,3,2,1,0:T(8,128)(2,1)} copy(bf16[7,8,2,128,128]{3,4,1,2,0:T(8,128)(2,1)} %convert_bitcast_fusion) | data formatting | bytes 7340032 | tf_op jit(solution)/shard_map/convert_element_type | solution.py:30
  166.0 3.0 broadcast_in_dim.8
  169.0 11.6 %scatter_fusion = bf16[64,2,128,128]{3,2,1,0:T(8,128)(2,1)} fusion(bf16[64,2,128,128]{3,2,1,0:T(8,128)(2,1)} %broadcast_in_dim.8, s32[56]{0:T(128)S(1)} %fusion.13, bf16[56,2,128,128]{3,2,1,0:T(8,128)(2,1)} %bitcast.77), kind=kCustom, calls=%fused_computation.1 | custom fusion | bytes 11010272 | tf_op jit(solution)/shard_map/scatter | solution.py:42
  180.6 195.5 %all_to_all.5 = bf16[32,2,2,128,128]{4,3,2,1,0:T(8,128)(2,1)S(1)} all-to-all(bf16[32,2,2,128,128]{4,3,2,1,0:T(8,128)(2,1)} %bitcast.76), channel_id=1, replica_groups=mesh['dp'=32,'tensor'=16] {'dp'}, dimensions={0} | all-to-all | bytes 8388608 | tf_op jit(solution)/shard_map/all_to_all | solution.py:43
  376.0 1.5 convert_reduce_fusion
  (5 shorter events, 0.0 us)
Async XLA Ops:
  6.5 140.3 %copy-start = (bf16[7,8,128,128]{3,2,1,0:T(8,128)(2,1)S(1)}, bf16[7,8,128,128]{3,2,1,0:T(8,128)(2,1)}, u32[]{:S(2)}) copy-start(bf16[7,8,128,128]{3,2,1,0:T(8,128)(2,1)} %param.8) | copy-start | bytes 5505028
  6.5 126.4 %all-gather.2.cloned.1.call-start = ((), (), s32[]{:S(2)}) async-start(), calls=%async_computation.1 | async-start | bytes 4456448 | tf_op jit(solution)/shard_map/all_gather | solution.py:13
  10.7 1.6 copy-start.3
  146.8 5.3 %copy-start.1 = (f32[512,7,128]{2,0,1:T(8,128)S(1)}, f32[512,7,128]{2,0,1:T(8,128)}, u32[]{:S(2)}) copy-start(f32[512,7,128]{2,0,1:T(8,128)} %copy.24) | copy-start | bytes 5505028
  146.9 5.8 %copy-start.2 = (bf16[56,512,128]{2,1,0:T(8,128)(2,1)S(1)}, bf16[56,512,128]{2,1,0:T(8,128)(2,1)}, u32[]{:S(2)}) copy-start(bf16[56,512,128]{2,1,0:T(8,128)(2,1)} %gather_fusion) | copy-start | bytes 22020100
  152.2 1.6 copy-start.4
Sparse Core Ops, SparseCore 0:
  10.6 122.2 all-gather.1
where the time goes:
time: 385 us; the launch traced here: 384 us
  blocking collectives  195 us (51%)
  waiting for transfers between devices  120 us (31%)
  local copies, waits for them, and re-layouts  41 us (11%)
  between operations  13.5 us (4%)
  matrix products  11.3 us (3%)
    all_to_all x1, blocking collectives, body(): lax.all_to_all(packed.reshape(owner_count, capacity, 2, block_size, block...  195 us
    all_gather x1, waiting for transfers between devices, body(): gathered = lax.all_gather(x_panel, 'tensor', axis=1, tiled=True)  120 us
    scatter x1, local copies, waits for them, and re-layouts, body(): packed.at[target]  11.6 us
  transfers between devices with their start and end apart: 1, of which 1 were waited for; matrix products, arithmetic and copies ran while one was open for 1% of the time, Pallas kernels for 0%

commit v1 on v0

--- a/solution.py
+++ b/solution.py
@@ -10,7 +10,8 @@
 
 
 def body(x_panel, grad_hidden, gate_blocks, up_blocks, block_rows, block_owner):
-    gathered = lax.all_gather(x_panel, "tensor", axis=1, tiled=True)
+    sent = jnp.stack([x_panel] * lax.axis_size("tensor"))
+    gathered = jnp.concatenate(lax.all_to_all(sent, "tensor", 0, 0), axis=1)
     token_count = gathered.shape[0]
     column_count = gate_blocks.shape[0]
     depth = gate_blocks.shape[1]

time: 385 us -> 471 us (1.22)
  blocking collectives: 195 us -> 323 us
  waiting for transfers between devices: 120 us -> 73.2 us
  starting transfers between devices: 0.01 us -> 18.3 us
  between operations: 13.5 us -> 0.11 us
    all_to_all x1, blocking collectives: 195 us -> 323 us  [body(): lax.all_to_all(packed.reshape(owner_count, capacity, 2, block_size, block...]
    all_gather x1 -> x0, waiting for transfers between devices: 120 us -> none  [body(): gathered = lax.all_gather(x_panel, 'tensor', axis=1, tiled=True)]
    all_to_all x0 -> x1, waiting for transfers between devices: none -> 73.2 us  [body(): gathered = jnp.concatenate(lax.all_to_all(sent, 'tensor', 0, 0), axis=1)]
    all_to_all x0 -> x1, starting transfers between devices: none -> 18.3 us  [body(): gathered = jnp.concatenate(lax.all_to_all(sent, 'tensor', 0, 0), axis=1)]
    another operation x0 -> x2, local copies, waits for them, and re-layouts: none -> 8.83 us  [the longest x1 6.45 us: body(): gathered.reshape(token_count, row_total, block_size)[:, block_rows, :]]
    reshape x1 -> x0, local copies, waits for them, and re-layouts: 6.45 us -> none  [body(): gathered.reshape(token_count, row_total, block_size)[:, block_rows, :]]
where the time goes in v1:
time: 471 us; the launch traced here: 470 us
  blocking collectives  323 us (69%)
  waiting for transfers between devices  73.2 us (16%)
  local copies, waits for them, and re-layouts  42.7 us (9%)
  starting transfers between devices  18.3 us (4%)
  matrix products  11.3 us (2%)
    all_to_all x1, blocking collectives, body(): lax.all_to_all(packed.reshape(owner_count, capacity, 2, block_size, block...  323 us
    all_to_all x1, waiting for transfers between devices, body(): gathered = jnp.concatenate(lax.all_to_all(sent, 'tensor', 0, 0), axis=1)  73.2 us
    all_to_all x1, starting transfers between devices, body(): gathered = jnp.concatenate(lax.all_to_all(sent, 'tensor', 0, 0), axis=1)  18.3 us
    scatter x1, local copies, waits for them, and re-layouts, body(): packed.at[target]  11.6 us
  transfers between devices with their start and end apart: 1, of which 1 were waited for; matrix products, arithmetic and copies ran while one was open for 1% of the time, Pallas kernels for 0%

profile of v1, /device:TPU:8, one launch (start us, length us, event | category | flops | bytes accessed | tf_op | source)
XLA Modules:
  0.0 470.5 jit_solution(4421788211905937213)
XLA Ops:
  0.0 0.0 copy-start
  0.0 1.2 copy.16
  1.2 2.4 stack.8
  3.6 18.3 %all-to-all-start = ((bf16[16,512,256]{1,2,0:T(8,128)(2,1)}), bf16[16,512,256]{1,2,0:T(8,128)(2,1)}, u32[]{:S(2)}, u32[]{:S(2)}) async-start(bf16[16,512,256]{1,2,0:T(8,128)(2,1)} %stack.8), calls=%async_computation | async-start | bytes 8388608 | tf_op jit(solution)/shard_map/all_to_all | solution.py:14
  21.9 0.0 copy-done.4
  21.9 0.1 reshape.54
  22.0 1.5 copy.15
  23.5 0.0 copy-start.3
  23.5 1.6 copy.18
  25.1 0.0 copy-done.3
  25.1 0.1 eq.15
  25.2 0.1 mul.39
  25.3 0.1 fusion.12
  25.3 0.1 reduce_window_sum.11
  25.4 0.2 select_reduce_fusion
  25.6 73.2 %all-to-all-done = bf16[16,512,256]{1,2,0:T(8,128)(2,1)} async-done(((bf16[16,512,256]{1,2,0:T(8,128)(2,1)}), bf16[16,512,256]{1,2,0:T(8,128)(2,1)}, u32[]{:S(2)}, u32[]{:S(2)}) %all-to-all-start) | async-done | bytes 4194336 | tf_op jit(solution)/shard_map/all_to_all | solution.py:14
  98.8 6.5 %copy.17 = bf16[512,32,128]{2,0,1:T(8,128)(2,1)} copy(bf16[512,32,128]{0,2,1:T(8,128)(2,1)} %bitcast.4) | data formatting | bytes 8388608 | tf_op jit(solution)/shard_map/reshape;reshape | solution.py:20
  105.3 7.4 %gather_fusion = bf16[56,512,128]{2,1,0:T(8,128)(2,1)} fusion(bf16[512,32,128]{2,0,1:T(8,128)(2,1)} %copy.17, s32[1024]{0:T(1024)S(1)} %pad_clamp_fusion), kind=kCustom, calls=%fused_computation | custom fusion | bytes 14680288 | tf_op jit(solution)/shard_map/gather | solution.py:20
  112.7 0.0 copy-done
  112.7 5.3 %fusion.14 = f32[7,512,128,1]{2,1,3,0:T(8,128)S(1)} fusion(bf16[512,7,8,128]{3,0,2,1:T(8,128)(2,1)} %bitcast.80, bf16[7,8,128,128]{3,2,1,0:T(8,128)(2,1)S(1)} %copy-done), kind=kOutput, calls=%fused_computation.30 | convolution fusion | flops 939524096 | bytes 11010048 | tf_op jit(solution)/shard_map/tckb,ckbe->tce/dot_general | solution.py:21
  118.0 0.0 copy-done.1
  118.0 0.0 copy-start.5
  118.0 0.5 fusion.11
  118.5 0.0 copy-done.2
  118.5 1.1 copy-done.5
  119.6 2.1 fusion.10
  121.8 3.9 convert_bitcast_fusion
  125.7 6.2 %copy.21 = bf16[7,8,2,128,128]{4,3,2,1,0:T(8,128)(2,1)} copy(bf16[7,8,2,128,128]{3,4,1,2,0:T(8,128)(2,1)} %convert_bitcast_fusion) | data formatting | bytes 7340032 | tf_op jit(solution)/shard_map/convert_element_type | solution.py:31
  131.9 3.0 broadcast_in_dim.8
  134.9 11.6 %scatter_fusion = bf16[64,2,128,128]{3,2,1,0:T(8,128)(2,1)} fusion(bf16[64,2,128,128]{3,2,1,0:T(8,128)(2,1)} %broadcast_in_dim.8, s32[56]{0:T(128)S(1)} %fusion.13, bf16[56,2,128,128]{3,2,1,0:T(8,128)(2,1)} %bitcast.79), kind=kCustom, calls=%fused_computation.1 | custom fusion | bytes 11010272 | tf_op jit(solution)/shard_map/scatter | solution.py:43
  146.4 322.6 %all_to_all.10 = bf16[32,2,2,128,128]{4,3,2,1,0:T(8,128)(2,1)S(1)} all-to-all(bf16[32,2,2,128,128]{4,3,2,1,0:T(8,128)(2,1)} %bitcast.78), channel_id=1, replica_groups=mesh['dp'=32,'tensor'=16] {'dp'}, dimensions={0} | all-to-all | bytes 8388608 | tf_op jit(solution)/shard_map/all_to_all | solution.py:44
  469.0 1.5 convert_reduce_fusion
  (7 shorter events, 0.0 us)
Async XLA Ops:
  0.0 112.7 %copy-start = (bf16[7,8,128,128]{3,2,1,0:T(8,128)(2,1)S(1)}, bf16[7,8,128,128]{3,2,1,0:T(8,128)(2,1)}, u32[]{:S(2)}) copy-start(bf16[7,8,128,128]{3,2,1,0:T(8,128)(2,1)} %param.8) | copy-start | bytes 5505028
  3.6 18.3 %copy-start.4 = (s32[7,8]{1,0:T(8,128)S(1)}, s32[7,8]{1,0:T(8,128)}, u32[]{:S(2)}) copy-start(s32[7,8]{1,0:T(8,128)} %param.10) | copy-start | bytes 676
  3.6 95.2 %all-to-all-start = ((bf16[16,512,256]{1,2,0:T(8,128)(2,1)}), bf16[16,512,256]{1,2,0:T(8,128)(2,1)}, u32[]{:S(2)}, u32[]{:S(2)}) async-start(bf16[16,512,256]{1,2,0:T(8,128)(2,1)} %stack.8), calls=%async_computation | async-start | bytes 8388608 | tf_op jit(solution)/shard_map/all_to_all | solution.py:14
  23.5 1.6 copy-start.3
  112.7 5.3 %copy-start.1 = (f32[512,7,128]{2,0,1:T(8,128)S(1)}, f32[512,7,128]{2,0,1:T(8,128)}, u32[]{:S(2)}) copy-start(f32[512,7,128]{2,0,1:T(8,128)} %copy.18) | copy-start | bytes 5505028
  112.7 5.8 %copy-start.2 = (bf16[56,512,128]{2,1,0:T(8,128)(2,1)S(1)}, bf16[56,512,128]{2,1,0:T(8,128)(2,1)}, u32[]{:S(2)}) copy-start(bf16[56,512,128]{2,1,0:T(8,128)(2,1)} %gather_fusion) | copy-start | bytes 22020100
  118.0 1.6 copy-start.5
